TPU v7x, 32 devices: a whole 2x2x4 slice. The times are simulated.
32 devices in a mesh: parts: 2 (over y), expert: 4 (over z), dp: 4 (over x, core), sub: 1.
Axes of the slice: x: 2, y: 2, z: 4, core: 2. Of those that a mesh axis runs over, the one named last changes fastest.
Arguments:
- tokens: bfloat16 [4096, 1024], P(('parts', 'expert', 'dp', 'sub')), parts along dimension 0, may hold values from -6 to 6
- expert_choice: int32 [4096, 1], P(('parts', 'expert', 'dp', 'sub')), parts along dimension 0, may hold values from 0 to 3; in each aligned block of 128 rows (0 to 127, 128 to 255, ...) at most 48 rows name the same one
- gate_prob: float32 [4096, 1], P(('parts', 'expert', 'dp', 'sub')), parts along dimension 0, may hold values from 0.1 to 1
- cotangent: bfloat16 [4096, 1024], P(('parts', 'expert', 'dp', 'sub')), parts along dimension 0, may hold values from -6 to 6
- w_gate: bfloat16 [4, 768, 1024], P('expert', 'sub'), may hold values from -0.1875 to 0.1875
- w_up: bfloat16 [4, 768, 1024], P('expert', 'sub'), may hold values from -0.1875 to 0.1875
- w_down: bfloat16 [4, 768, 1024], P('expert', 'sub'), may hold values from -0.21875 to 0.21875
Outputs:
- layer_out: bfloat16 [4096, 1024], P(('parts', 'expert', 'dp', 'sub')), parts along dimension 0
- d_tokens: bfloat16 [4096, 1024], P(('parts', 'expert', 'dp', 'sub')), parts along dimension 0
- d_gate: float32 [4096, 1], P(('parts', 'expert', 'dp', 'sub')), parts along dimension 0
- d_w_gate: bfloat16 [8, 768, 1024], P(('parts', 'expert'), 'sub', 'dp'), parts along dimension 0
- d_w_up: bfloat16 [8, 768, 1024], P(('parts', 'expert'), 'sub', 'dp'), parts along dimension 0
- d_w_down: bfloat16 [8, 768, 1024], P(('parts', 'expert'), 'sub', 'dp'), parts along dimension 0
There are 2 independent parts, one for each index of `parts`. A program takes and returns all parts, laid end to end along the dimension named above; an argument that names none is the same for every part. Nothing has to cross between parts.
Inputs may be any that keep to these rules, and one draw needn't show every extreme that they name: `expert_choice`: each row names one expert. Within the tokens of one device (aligned blocks of 128 rows), no expert is named by more than 48 rows, and in every draw some expert is named by exactly 48 rows of some block.
All inputs are finite; a program needn't handle non-finite values.
Results may differ from a plain program's by a relative error of at most 0.017.
Values may be sent and summed in bfloat16 or wider, within the bound.
A program may use at most 64 MiB of HBM per device.

v0:
```python
import jax
import jax.numpy as jnp
from jax import lax
from jax.sharding import PartitionSpec as P


def contract_last(left, right):
    return lax.dot_general(
        left, right, (((1,), (1,)), ((), ())), preferred_element_type=jnp.float32
    )


def contract_rows(left, right):
    return lax.dot_general(
        left, right, (((0,), (0,)), ((), ())), preferred_element_type=jnp.float32
    )


def local(tokens, expert_choice, gate_prob, cotangent, w_gate, w_up, w_down):
    n_expert = lax.axis_size("expert")
    tok_rows, feature_width = tokens.shape
    top_count = expert_choice.shape[1]
    pair_count = tok_rows * top_count
    capacity = 3 * pair_count // (2 * n_expert)
    slot_total = n_expert * capacity
    flat_choice = expert_choice.reshape(pair_count)
    onehot = (flat_choice[:, None] == jnp.arange(n_expert, dtype=jnp.int32)[None, :]).astype(
        jnp.int32
    )
    before = jnp.cumsum(onehot, axis=0) - onehot
    position = jnp.sum(before * onehot, axis=1)
    slot_index = flat_choice * capacity + position
    selector = (slot_index[None, :] == jnp.arange(slot_total, dtype=jnp.int32)[:, None]).astype(
        jnp.bfloat16
    )
    x_pairs = jnp.repeat(tokens, top_count, axis=0)
    cot_pairs = jnp.repeat(cotangent, top_count, axis=0)
    dy_pairs = (gate_prob * cot_pairs.astype(jnp.float32)).astype(jnp.bfloat16)
    x_send = jnp.dot(selector, x_pairs, preferred_element_type=jnp.float32).astype(jnp.bfloat16)
    dy_send = jnp.dot(selector, dy_pairs, preferred_element_type=jnp.float32).astype(jnp.bfloat16)
    weight_gate = w_gate[0]
    weight_up = w_up[0]
    weight_down = w_down[0]
    x_recv, dy_recv = (
        lax.all_to_all(x_send, "expert", split_axis=0, concat_axis=0, tiled=True),
        lax.all_to_all(dy_send, "expert", split_axis=0, concat_axis=0, tiled=True),
    )
    x_rows, dy_rows = (
        lax.all_gather(x_recv, "sub", axis=0, tiled=True),
        lax.all_gather(dy_recv, "sub", axis=0, tiled=True),
    )
    gate_pre = contract_last(x_rows, weight_gate)
    up_pre = contract_last(x_rows, weight_up)
    sigmoid_gate = jax.nn.sigmoid(gate_pre)
    activated = gate_pre * sigmoid_gate
    silu_slope = sigmoid_gate * (1.0 + gate_pre * (1.0 - sigmoid_gate))
    hidden = (activated * up_pre).astype(jnp.bfloat16)
    out_part = jnp.dot(hidden, weight_down, preferred_element_type=jnp.float32)
    d_hidden = contract_last(dy_rows, weight_down)
    grad_down = contract_rows(hidden, dy_rows)
    d_gate_pre = (d_hidden * up_pre * silu_slope).astype(jnp.bfloat16)
    d_up_pre = (d_hidden * activated).astype(jnp.bfloat16)
    dx_part = jnp.dot(d_gate_pre, weight_gate, preferred_element_type=jnp.float32) + jnp.dot(
        d_up_pre, weight_up, preferred_element_type=jnp.float32
    )
    grad_gate = contract_rows(d_gate_pre, x_rows)
    grad_up = contract_rows(d_up_pre, x_rows)
    summed_gate = lax.psum_scatter(
        grad_gate.astype(jnp.bfloat16), "dp", scatter_dimension=1, tiled=True
    ).astype(jnp.float32)
    summed_up = lax.psum_scatter(
        grad_up.astype(jnp.bfloat16), "dp", scatter_dimension=1, tiled=True
    ).astype(jnp.float32)
    summed_down = lax.psum_scatter(
        grad_down.astype(jnp.bfloat16), "dp", scatter_dimension=1, tiled=True
    ).astype(jnp.float32)
    out_part, dx_part, summed = (out_part, dx_part, (summed_gate, summed_up, summed_down))
    out_mine, dx_mine = (
        lax.psum_scatter(
            out_part.astype(jnp.bfloat16), "sub", scatter_dimension=0, tiled=True
        ).astype(jnp.float32),
        lax.psum_scatter(
            dx_part.astype(jnp.bfloat16), "sub", scatter_dimension=0, tiled=True
        ).astype(jnp.float32),
    )
    out_back, dx_back = (
        lax.all_to_all(
            out_mine.astype(jnp.bfloat16), "expert", split_axis=0, concat_axis=0, tiled=True
        ),
        lax.all_to_all(
            dx_mine.astype(jnp.bfloat16), "expert", split_axis=0, concat_axis=0, tiled=True
        ),
    )
    out_three = contract_rows(selector, out_back).reshape(tok_rows, top_count, feature_width)
    dx_three = contract_rows(selector, dx_back).reshape(tok_rows, top_count, feature_width)
    layer_out = jnp.sum(gate_prob[:, :, None] * out_three, axis=1).astype(jnp.bfloat16)
    d_gate = jnp.sum(out_three * cotangent[:, None, :].astype(jnp.float32), axis=2)
    d_tokens = jnp.sum(dx_three, axis=1).astype(jnp.bfloat16)
    summed_gate, summed_up, summed_down = summed
    return (
        layer_out,
        d_tokens,
        d_gate,
        summed_gate.astype(jnp.bfloat16)[None],
        summed_up.astype(jnp.bfloat16)[None],
        summed_down.astype(jnp.bfloat16)[None],
    )


def solution(mesh):
    in_specs = (
        P(("parts", "expert", "dp", "sub"), None),
        P(("parts", "expert", "dp", "sub"), None),
        P(("parts", "expert", "dp", "sub"), None),
        P(("parts", "expert", "dp", "sub"), None),
        P("expert", "sub", None),
        P("expert", "sub", None),
        P("expert", "sub", None),
    )
    out_specs = (
        P(("parts", "expert", "dp", "sub"), None),
        P(("parts", "expert", "dp", "sub"), None),
        P(("parts", "expert", "dp", "sub"), None),
        P(("parts", "expert"), "sub", "dp"),
        P(("parts", "expert"), "sub", "dp"),
        P(("parts", "expert"), "sub", "dp"),
    )
    return jax.shard_map(local, mesh=mesh, in_specs=in_specs, out_specs=out_specs, check_vma=False)
```

profile of v0, /device:TPU:0, one launch (start us, length us, event | category | flops | bytes accessed | tf_op | source)
XLA Modules:
  0.0 147.7 jit_solution(10316610326050013642)
XLA Ops:
  7.2 0.9 fusion.27
  8.1 0.2 reduce_window_sum.11
  8.2 0.8 select_reduce_fusion
  9.1 0.7 multiply_add_fusion
  9.7 2.0 %convolution_convert_fusion.4 = bf16[192,1024]{1,0:T(8,128)(2,1)} fusion(bf16[128,1024]{1,0:T(8,128)(2,1)} %param.7, s32[128]{0:T(128)S(1)} %multiply_add_fusion), kind=kOutput, calls=%fused_computation.19 | convolution fusion | flops 50552832 | bytes 655872 | tf_op jit(solution)/shard_map/dot_general | solution.py:39
  11.7 6.3 %all-to-all-start = ((bf16[4,48,1024]{2,1,0:T(8,128)(2,1)}), bf16[4,48,1024]{2,1,0:T(8,128)(2,1)S(1)}, u32[]{:S(2)}, u32[]{:S(2)}) async-start(bf16[4,48,1024]{2,1,0:T(8,128)(2,1)} %bitcast.2), calls=%async_computation | async-start | bytes 786432 | tf_op jit(solution)/shard_map/all_to_all | solution.py:45
  18.0 1.1 convolution_convert_fusion.3
  19.1 10.6 %all-to-all-done = bf16[4,48,1024]{2,1,0:T(8,128)(2,1)S(1)} async-done(((bf16[4,48,1024]{2,1,0:T(8,128)(2,1)}), bf16[4,48,1024]{2,1,0:T(8,128)(2,1)S(1)}, u32[]{:S(2)}, u32[]{:S(2)}) %all-to-all-start) | async-done | bytes 393248 | tf_op jit(solution)/shard_map/all_to_all | solution.py:45
  29.7 4.2 %all-to-all-start.2 = ((bf16[4,48,1024]{2,1,0:T(8,128)(2,1)}), bf16[4,48,1024]{2,1,0:T(8,128)(2,1)}, u32[]{:S(2)}, u32[]{:S(2)}) async-start(bf16[4,48,1024]{2,1,0:T(8,128)(2,1)} %bitcast.58), calls=%async_computation.2 | async-start | bytes 786432 | tf_op jit(solution)/shard_map/all_to_all | solution.py:46
  33.9 0.0 reduce-scatter.4.cloned.1.call-start
  34.0 2.9 %fusion.6 = f32[192,768]{1,0:T(8,128)} fusion(bf16[192,1024]{1,0:T(8,128)(2,1)S(1)} %bitcast.53, bf16[1,768,1024]{2,1,0:T(8,128)(2,1)} %param.12), kind=kOutput, calls=%fused_computation.9 | convolution fusion | flops 301989888 | bytes 2555904 | tf_op jit(solution)/shard_map/dot_general | solution.py:8
  36.9 8.0 %all-to-all-done.2 = bf16[4,48,1024]{2,1,0:T(8,128)(2,1)} async-done(((bf16[4,48,1024]{2,1,0:T(8,128)(2,1)}), bf16[4,48,1024]{2,1,0:T(8,128)(2,1)}, u32[]{:S(2)}, u32[]{:S(2)}) %all-to-all-start.2) | async-done | bytes 393248 | tf_op jit(solution)/shard_map/all_to_all | solution.py:46
  44.9 1.7 %fusion = f32[192,768]{1,0:T(8,128)S(1)} fusion(bf16[192,1024]{1,0:T(8,128)(2,1)} %bitcast.10, bf16[1,768,1024]{2,1,0:T(8,128)(2,1)S(1)} %copy-done.1), kind=kOutput, calls=%fused_computation.3 | convolution fusion | flops 301989888 | bytes 2555904 | tf_op jit(solution)/shard_map/dot_general | solution.py:8
  46.7 1.8 %multiply_convert_fusion.1 = (bf16[192,768]{1,0:T(8,128)(2,1)S(1)}, bf16[192,768]{1,0:T(8,128)(2,1)}, bf16[192,768]{1,0:T(8,128)(2,1)}) fusion(f32[192,768]{1,0:T(8,128)S(1)} %fusion, f32[192,768]{1,0:T(8,128)S(1)} %copy-done.7, bf16[192,1024]{1,0:T(8,128)(2,1)S(1)} %bitcast.54, bf16[1,768,1024]{2,1,0:T(8,128)(2,1)S(1)} %copy-done), kind=kOutput, calls=%fused_computation.24 | convolution fusion | flops 304201728 | bytes 4030464 | tf_op jit(solution)/shard_map/dot_general | solution.py:8
  48.4 0.7 copy-done.3
  49.1 1.8 %convolution_convert_fusion.2 = bf16[768,1024]{1,0:T(8,128)(2,1)} fusion(bf16[192,768]{1,0:T(8,128)(2,1)S(1)} %get-tuple-element.6, bf16[192,1024]{1,0:T(8,128)(2,1)S(1)} %bitcast.55), kind=kOutput, calls=%fused_computation.2 | convolution fusion | flops 302776320 | bytes 2260992 | tf_op jit(solution)/shard_map/dot_general | solution.py:14
  50.9 0.0 reduce-scatter.6.cloned.1.call-start
  51.0 2.7 %convolution_convert_fusion.1 = bf16[768,1024]{1,0:T(8,128)(2,1)} fusion(bf16[192,768]{1,0:T(8,128)(2,1)} %get-tuple-element.7, bf16[192,1024]{1,0:T(8,128)(2,1)S(1)} %bitcast.56), kind=kOutput, calls=%fused_computation.1 | convolution fusion | flops 302776320 | bytes 2260992 | tf_op jit(solution)/shard_map/dot_general | solution.py:14
  53.8 0.9 copy-done.2
  54.7 2.9 %convolution_convert_fusion = bf16[768,1024]{1,0:T(8,128)(2,1)} fusion(bf16[192,768]{1,0:T(8,128)(2,1)S(1)} %copy-done.2, bf16[192,1024]{1,0:T(8,128)(2,1)} %bitcast.10), kind=kOutput, calls=%fused_computation | convolution fusion | flops 302776320 | bytes 2260992 | tf_op jit(solution)/shard_map/dot_general | solution.py:14
  57.5 1.0 copy-done.5
  58.5 2.0 %fusion.4 = f32[192,1024]{1,0:T(8,128)S(1)} fusion(bf16[192,768]{1,0:T(8,128)(2,1)S(1)} %copy-done.5, bf16[1,768,1024]{2,1,0:T(8,128)(2,1)} %param.12), kind=kOutput, calls=%fused_computation.7 | convolution fusion | flops 301989888 | bytes 2654208 | tf_op jit(solution)/shard_map/dot_general | solution.py:63
  60.5 1.3 fusion.15
  61.8 3.5 %all-to-all-start.3 = ((bf16[4,48,1024]{2,1,0:T(8,128)(2,1)}), bf16[4,48,1024]{2,1,0:T(8,128)(2,1)S(1)}, u32[]{:S(2)}, u32[]{:S(2)}) async-start(bf16[4,48,1024]{2,1,0:T(8,128)(2,1)} %bitcast.59), calls=%async_computation.3 | async-start | bytes 786432 | tf_op jit(solution)/shard_map/all_to_all | solution.py:90
  65.2 2.2 %fusion.18 = bf16[192,1024]{1,0:T(8,128)(2,1)} fusion(bf16[192,768]{1,0:T(8,128)(2,1)} %get-tuple-element.8, bf16[1,768,1024]{2,1,0:T(8,128)(2,1)S(1)} %copy-done.1), kind=kOutput, calls=%fused_computation.17 | convolution fusion | flops 302186496 | bytes 2260992 | tf_op jit(solution)/shard_map/dot_general | solution.py:58
  67.4 7.7 %all-to-all-done.3 = bf16[4,48,1024]{2,1,0:T(8,128)(2,1)S(1)} async-done(((bf16[4,48,1024]{2,1,0:T(8,128)(2,1)}), bf16[4,48,1024]{2,1,0:T(8,128)(2,1)S(1)}, u32[]{:S(2)}, u32[]{:S(2)}) %all-to-all-start.3) | async-done | bytes 393248 | tf_op jit(solution)/shard_map/all_to_all | solution.py:90
  75.1 3.5 %all-to-all-start.1 = ((bf16[4,48,1024]{2,1,0:T(8,128)(2,1)}), bf16[4,48,1024]{2,1,0:T(8,128)(2,1)S(1)}, u32[]{:S(2)}, u32[]{:S(2)}) async-start(bf16[4,48,1024]{2,1,0:T(8,128)(2,1)} %bitcast.61), calls=%async_computation.1 | async-start | bytes 786432 | tf_op jit(solution)/shard_map/all_to_all | solution.py:87
  78.6 1.0 convolution_convert_fusion.5
  79.5 8.8 %all-to-all-done.1 = bf16[4,48,1024]{2,1,0:T(8,128)(2,1)S(1)} async-done(((bf16[4,48,1024]{2,1,0:T(8,128)(2,1)}), bf16[4,48,1024]{2,1,0:T(8,128)(2,1)S(1)}, u32[]{:S(2)}, u32[]{:S(2)}) %all-to-all-start.1) | async-done | bytes 393248 | tf_op jit(solution)/shard_map/all_to_all | solution.py:87
  88.3 2.6 %fusion.23 = (f32[128]{0:T(128)}, bf16[128,1024]{1,0:T(8,128)(2,1)}) fusion(bf16[128,1024]{1,0:T(8,128)(2,1)} %param.10, f32[128]{0:T(128)S(1)} %bitcast.65, bf16[192,1024]{1,0:T(8,128)(2,1)S(1)} %bitcast.60, s32[128]{0:T(128)S(1)} %multiply_add_fusion), kind=kOutput, calls=%fused_computation.29 | convolution fusion | flops 51011456 | bytes 919040 | tf_op jit(solution)/shard_map/dot_general | solution.py:14
  90.9 18.9 %reduce-scatter.6.cloned.1.call-done = bf16[768,256]{1,0:T(8,128)(2,1)} async-done(((bf16[768,1024]{1,0:T(8,128)(2,1)}), bf16[768,256]{1,0:T(8,128)(2,1)}) %reduce-scatter.6.cloned.1.call-update) | async-done | bytes 393232 | tf_op jit(solution)/shard_map/reduce_scatter | solution.py:71
  109.8 31.3 %reduce-scatter.8.cloned.1.call-done = bf16[768,256]{1,0:T(8,128)(2,1)} async-done(((bf16[768,1024]{1,0:T(8,128)(2,1)}), bf16[768,256]{1,0:T(8,128)(2,1)}) %reduce-scatter.8.cloned.1.call-update) | async-done | bytes 393232 | tf_op jit(solution)/shard_map/reduce_scatter | solution.py:74
  (20 shorter events, 0.1 us)
Async XLA Ops:
  7.2 39.5 %copy-start = (bf16[1,768,1024]{2,1,0:T(8,128)(2,1)S(1)}, bf16[1,768,1024]{2,1,0:T(8,128)(2,1)}, u32[]{:S(2)}) copy-start(bf16[1,768,1024]{2,1,0:T(8,128)(2,1)} %param.11) | copy-start | bytes 4718596
  7.2 10.8 %copy-start.8 = (f32[128,1]{0,1:T(1,128)S(1)}, f32[128,1]{0,1:T(1,128)}, u32[]{:S(2)}) copy-start(f32[128,1]{0,1:T(1,128)} %param.9) | copy-start | bytes 1540
  7.2 10.8 %copy-start.6 = (bf16[128,1024]{1,0:T(8,128)(2,1)S(1)}, bf16[128,1024]{1,0:T(8,128)(2,1)}, u32[]{:S(2)}) copy-start(bf16[128,1024]{1,0:T(8,128)(2,1)} %param.10) | copy-start | bytes 786436
  11.7 18.0 %all-to-all-start = ((bf16[4,48,1024]{2,1,0:T(8,128)(2,1)}), bf16[4,48,1024]{2,1,0:T(8,128)(2,1)S(1)}, u32[]{:S(2)}, u32[]{:S(2)}) async-start(bf16[4,48,1024]{2,1,0:T(8,128)(2,1)} %bitcast.2), calls=%async_computation | async-start | bytes 786432 | tf_op jit(solution)/shard_map/all_to_all | solution.py:45
  29.7 15.2 %copy-start.1 = (bf16[1,768,1024]{2,1,0:T(8,128)(2,1)S(1)}, bf16[1,768,1024]{2,1,0:T(8,128)(2,1)}, u32[]{:S(2)}) copy-start(bf16[1,768,1024]{2,1,0:T(8,128)(2,1)} %param.13) | copy-start | bytes 4718596
  29.7 15.2 %all-to-all-start.2 = ((bf16[4,48,1024]{2,1,0:T(8,128)(2,1)}), bf16[4,48,1024]{2,1,0:T(8,128)(2,1)}, u32[]{:S(2)}, u32[]{:S(2)}) async-start(bf16[4,48,1024]{2,1,0:T(8,128)(2,1)} %bitcast.58), calls=%async_computation.2 | async-start | bytes 786432 | tf_op jit(solution)/shard_map/all_to_all | solution.py:46
  33.9 57.0 %reduce-scatter.4.cloned.1.call-start = ((), (), s32[]{:S(2)}) async-start(), calls=%async_computation.7 | async-start | bytes 1966080 | tf_op jit(solution)/shard_map/reduce_scatter | solution.py:68
  44.9 1.7 %copy-start.7 = (f32[192,768]{1,0:T(8,128)S(1)}, f32[192,768]{1,0:T(8,128)}, u32[]{:S(2)}) copy-start(f32[192,768]{1,0:T(8,128)} %fusion.6) | copy-start | bytes 1769476
  48.4 0.7 copy-start.3
  50.9 58.9 %reduce-scatter.6.cloned.1.call-start = ((), (), s32[]{:S(2)}) async-start(), calls=%async_computation.8 | async-start | bytes 1966080 | tf_op jit(solution)/shard_map/reduce_scatter | solution.py:71
  53.7 1.0 copy-start.2
  53.7 87.4 %reduce-scatter.8.cloned.1.call-start = ((), (), s32[]{:S(2)}) async-start(), calls=%async_computation.9 | async-start | bytes 1966080 | tf_op jit(solution)/shard_map/reduce_scatter | solution.py:74
  57.5 1.0 copy-start.5
  58.5 2.0 %copy-start.4 = (bf16[192,768]{1,0:T(8,128)(2,1)S(1)}, bf16[192,768]{1,0:T(8,128)(2,1)}, u32[]{:S(2)}) copy-start(bf16[192,768]{1,0:T(8,128)(2,1)} %copy-done.3) | copy-start | bytes 884740
  61.8 13.3 %all-to-all-start.3 = ((bf16[4,48,1024]{2,1,0:T(8,128)(2,1)}), bf16[4,48,1024]{2,1,0:T(8,128)(2,1)S(1)}, u32[]{:S(2)}, u32[]{:S(2)}) async-start(bf16[4,48,1024]{2,1,0:T(8,128)(2,1)} %bitcast.59), calls=%async_computation.3 | async-start | bytes 786432 | tf_op jit(solution)/shard_map/all_to_all | solution.py:90
  75.1 13.2 %all-to-all-start.1 = ((bf16[4,48,1024]{2,1,0:T(8,128)(2,1)}), bf16[4,48,1024]{2,1,0:T(8,128)(2,1)S(1)}, u32[]{:S(2)}, u32[]{:S(2)}) async-start(bf16[4,48,1024]{2,1,0:T(8,128)(2,1)} %bitcast.61), calls=%async_computation.1 | async-start | bytes 786432 | tf_op jit(solution)/shard_map/all_to_all | solution.py:87
Sparse Core Ops, SparseCore 0:
  51.0 27.2 reduce-scatter.3
  81.6 28.1 reduce-scatter.5
  112.9 28.1 reduce-scatter.7
where the time goes:
time: 148 us
  waiting for transfers between devices  85.4 us (58%)
  matrix products  25.8 us (17%)
  starting transfers between devices  17.6 us (12%)
  between operations  13.9 us (9%)
  local copies, waits for them, and re-layouts  2.58 us (2%)
  other arithmetic  2.53 us (2%)
    reduce_scatter x1, waiting for transfers between devices, local(): lax.psum_scatter(grad_down.astype(jnp.bfloat16), 'dp', scatter_dimension=...  31.3 us
    reduce_scatter x1, waiting for transfers between devices, local(): lax.psum_scatter(grad_up.astype(jnp.bfloat16), 'dp', scatter_dimension=1,...  18.9 us
    dot_general x5, matrix products, contract_rows(): lax.dot_general(left, right, (((0,), (0,)), ((), ())), preferred_element_...  10.9 us
    all_to_all x1, waiting for transfers between devices, local(): lax.all_to_all(x_send, 'expert', split_axis=0, concat_axis=0, tiled=True)  10.6 us
    all_to_all x1, waiting for transfers between devices, local(): lax.all_to_all(out_mine.astype(jnp.bfloat16), 'expert', split_axis=0, con...  8.8 us
    all_to_all x1, waiting for transfers between devices, local(): lax.all_to_all(dy_send, 'expert', split_axis=0, concat_axis=0, tiled=True)  8.01 us
    all_to_all x1, waiting for transfers between devices, local(): lax.all_to_all(dx_mine.astype(jnp.bfloat16), 'expert', split_axis=0, conc...  7.67 us
    dot_general x3, matrix products, contract_last(): lax.dot_general(left, right, (((1,), (1,)), ((), ())), preferred_element_...  6.39 us
  transfers between devices with their start and end apart: 7, of which 6 were waited for; matrix products, arithmetic and copies ran while one was open for 13% of the time, Pallas kernels for 0%

commit v1 on v0

--- a/solution.py
+++ b/solution.py
@@ -1,6 +1,10 @@
+import functools
+
 import jax
 import jax.numpy as jnp
 from jax import lax
+from jax.experimental import pallas as pl
+from jax.experimental.pallas import tpu as pltpu
 from jax.sharding import PartitionSpec as P
 
 
@@ -107,6 +111,326 @@
     )
 
 
+LANES = 128
+BLOCK = 256
+MESH = pl.DeviceIdType.MESH
+
+
+def matmul(left, right):
+    return jnp.dot(left, right, preferred_element_type=jnp.float32)
+
+
+def kernel(
+    n, capacity,
+    tokens_ref, choice_ref, prob_ref, cot_ref, w_gate_hbm, w_up_hbm, w_down_hbm,
+    out_ref, dx_ref, d_gate_ref, grad_gate_ref, grad_up_ref, grad_down_ref,
+    w_gate, w_up, w_down, x_send, y_send, x_all, y_all,
+    active, slope, hidden, d_gate_pre, d_up_pre,
+    active_t, slope_t, hidden_t, out_rows, dx_rows, out_back, dx_back,
+    load_sem, go_sem, go_recv, fwd_sem, fwd_recv, back_sem, back_recv,
+):
+    me = lax.axis_index("expert")
+    dp = lax.axis_index("dp")
+    sibling = dp + 1 - 2 * lax.rem(dp, 2)
+    across = lax.rem(dp + 2, 4)
+    peers = [lax.rem(me + s, n) for s in range(n)]
+    sources = [lax.rem(me + n - s, n) for s in range(n)]
+    own = n * capacity
+    units = w_gate.shape[0]
+    features = w_gate.shape[1]
+    steps = range(1, n)
+
+    barrier = pltpu.get_barrier_semaphore()
+    for s in steps:
+        pl.semaphore_signal(barrier, inc=1, device_id={"expert": peers[s]}, device_id_type=MESH)
+    for d in (sibling, across):
+        pl.semaphore_signal(barrier, inc=1, device_id={"dp": d}, device_id_type=MESH)
+
+    loads = [
+        pltpu.make_async_copy(src, dst, load_sem.at[i])
+        for i, (src, dst) in enumerate(
+            ((w_gate_hbm, w_gate), (w_up_hbm, w_up), (w_down_hbm, w_down))
+        )
+    ]
+    for load in loads:
+        load.start()
+
+    choice = choice_ref[...]
+    relative = choice - me
+    relative = jnp.where(relative < 0, relative + n, relative)
+    tok = LANES
+    row_id = lax.broadcasted_iota(jnp.int32, (tok, tok), 0)
+    col_id = lax.broadcasted_iota(jnp.int32, (tok, tok), 1)
+    earlier = (row_id < col_id).astype(jnp.bfloat16)
+    expert_rows = max(16, n)
+    onehot = lax.broadcasted_iota(jnp.int32, (expert_rows, tok), 0) == relative
+    before = matmul(onehot.astype(jnp.bfloat16), earlier)
+    position = jnp.sum(jnp.where(onehot, before, 0.0), axis=0, keepdims=True)
+    slot = relative * capacity + position.astype(jnp.int32)
+    selector = (
+        lax.broadcasted_iota(jnp.int32, (own, tok), 0) == slot
+    ).astype(jnp.bfloat16)
+    diagonal = row_id == col_id
+    prob = jnp.sum(jnp.where(diagonal, prob_ref[...], 0.0), axis=1, keepdims=True)
+
+    def rows(s, group=0):
+        return pl.ds(group * own + s * capacity, capacity)
+
+    def dispatch(values, buffer, held, array):
+        picked = matmul(selector, values).astype(jnp.bfloat16)
+        held[pl.ds(0, capacity), :] = picked[:capacity]
+        buffer[...] = picked[capacity:]
+
+    def go(array, s):
+        buffer, held = ((x_send, x_all), (y_send, y_all))[array]
+        return pltpu.make_async_remote_copy(
+            src_ref=buffer.at[pl.ds((s - 1) * capacity, capacity)],
+            dst_ref=held.at[rows(s)],
+            send_sem=go_sem.at[array, s],
+            recv_sem=go_recv.at[array, s],
+            device_id={"expert": peers[s]},
+            device_id_type=MESH,
+        )
+
+    def forward(array, s, kind):
+        held = (x_all, y_all)[array]
+        came, lands, target = ((0, 1, sibling), (0, 2, across), (2, 3, sibling))[kind]
+        return pltpu.make_async_remote_copy(
+            src_ref=held.at[rows(s, came)],
+            dst_ref=held.at[rows(s, lands)],
+            send_sem=fwd_sem.at[array, kind, s],
+            recv_sem=fwd_recv.at[array, kind, s],
+            device_id={"dp": target},
+            device_id_type=MESH,
+        )
+
+    def back(array, s):
+        made, held = ((out_rows, out_back), (dx_rows, dx_back))[array]
+        return pltpu.make_async_remote_copy(
+            src_ref=made.at[rows(s)],
+            dst_ref=held.at[rows(s)],
+            send_sem=back_sem.at[array, s],
+            recv_sem=back_recv.at[array, s],
+            device_id={"expert": sources[s]},
+            device_id_type=MESH,
+        )
+
+    dispatch(tokens_ref[...], x_send, x_all, 0)
+    pl.semaphore_wait(barrier, n + 1)
+    for s in steps:
+        go(0, s).start()
+    forward(0, 0, 1).start()
+    forward(0, 0, 0).start()
+    scaled = (prob * cot_ref[...].astype(jnp.float32)).astype(jnp.bfloat16)
+    dispatch(scaled, y_send, y_all, 1)
+    for s in steps:
+        go(1, s).start()
+    forward(1, 0, 1).start()
+    forward(1, 0, 0).start()
+
+    tail = out_back.shape[0] - own
+    if tail:
+        out_back[pl.ds(own, tail), :] = jnp.zeros((tail, features), jnp.bfloat16)
+        dx_back[pl.ds(own, tail), :] = jnp.zeros((tail, features), jnp.bfloat16)
+    for load in loads:
+        load.wait()
+
+    for s in steps:
+        go(0, s).wait_recv()
+        forward(0, s, 1).start()
+        forward(0, s, 0).start()
+
+    def parts_of(gate_pre, up_pre):
+        sigmoid = jax.nn.sigmoid(gate_pre)
+        activated = gate_pre * sigmoid
+        sloped = up_pre * (sigmoid * (1.0 + gate_pre * (1.0 - sigmoid)))
+        return activated, sloped, (activated * up_pre).astype(jnp.bfloat16)
+
+    mine = pl.ds(0, own)
+
+    def own_forward(u, carry):
+        cut = pl.ds(pl.multiple_of(u * BLOCK, BLOCK), BLOCK)
+        x = x_all[mine, :]
+        activated, sloped, made = parts_of(
+            contract_last(x, w_gate[cut, :]), contract_last(x, w_up[cut, :])
+        )
+        active[:, cut] = activated
+        slope[:, cut] = sloped
+        hidden[:, cut] = made
+        return carry
+
+    lax.fori_loop(0, units // BLOCK, own_forward, 0)
+
+    def own_out(j, carry):
+        cut = pl.ds(pl.multiple_of(j * BLOCK, BLOCK), BLOCK)
+        out_rows[:, cut] = matmul(hidden[...], w_down[:, cut]).astype(jnp.bfloat16)
+        return carry
+
+    lax.fori_loop(0, features // BLOCK, own_out, 0)
+    for s in steps:
+        back(0, s).start()
+    out_back[pl.ds(0, capacity), :] = out_rows[pl.ds(0, capacity), :]
+
+    for s in range(n):
+        forward(0, s, 1).wait_recv()
+        forward(0, s, 2).start()
+    for kind in (0, 2):
+        for s in range(n):
+            forward(0, s, kind).wait_recv()
+
+    def all_forward(u, carry):
+        cut = pl.ds(pl.multiple_of(u * BLOCK, BLOCK), BLOCK)
+        x = x_all[...]
+        activated, sloped, made = parts_of(
+            contract_last(w_gate[cut, :], x), contract_last(w_up[cut, :], x)
+        )
+        active_t[cut, :] = activated
+        slope_t[cut, :] = sloped
+        hidden_t[cut, :] = made
+        return carry
+
+    lax.fori_loop(0, units // BLOCK, all_forward, 0)
+
+    for s in steps:
+        go(1, s).wait_recv()
+        forward(1, s, 1).start()
+        forward(1, s, 0).start()
+
+    def own_backward(u, carry):
+        cut = pl.ds(pl.multiple_of(u * BLOCK, BLOCK), BLOCK)
+        d_hidden = contract_last(y_all[mine, :], w_down[cut, :])
+        d_gate_pre[:, cut] = (d_hidden * slope[:, cut]).astype(jnp.bfloat16)
+        d_up_pre[:, cut] = (d_hidden * active[:, cut]).astype(jnp.bfloat16)
+        return carry
+
+    lax.fori_loop(0, units // BLOCK, own_backward, 0)
+
+    def own_dx(j, carry):
+        cut = pl.ds(pl.multiple_of(j * BLOCK, BLOCK), BLOCK)
+        dx_rows[:, cut] = (
+            matmul(d_gate_pre[...], w_gate[:, cut]) + matmul(d_up_pre[...], w_up[:, cut])
+        ).astype(jnp.bfloat16)
+        return carry
+
+    lax.fori_loop(0, features // BLOCK, own_dx, 0)
+    for s in steps:
+        back(1, s).start()
+    dx_back[pl.ds(0, capacity), :] = dx_rows[pl.ds(0, capacity), :]
+
+    for s in range(n):
+        forward(1, s, 1).wait_recv()
+        forward(1, s, 2).start()
+    for kind in (0, 2):
+        for s in range(n):
+            forward(1, s, kind).wait_recv()
+
+    width = grad_gate_ref.shape[1]
+    columns = pl.ds(pl.multiple_of(dp * width, width), width)
+
+    def all_backward(u, carry):
+        cut = pl.ds(pl.multiple_of(u * BLOCK, BLOCK), BLOCK)
+        d_hidden = contract_last(w_down[cut, :], y_all[...])
+        left_gate = (d_hidden * slope_t[cut, :]).astype(jnp.bfloat16)
+        left_up = (d_hidden * active_t[cut, :]).astype(jnp.bfloat16)
+        x = x_all[:, columns]
+        grad_gate_ref[cut, :] = matmul(left_gate, x).astype(jnp.bfloat16)
+        grad_up_ref[cut, :] = matmul(left_up, x).astype(jnp.bfloat16)
+        grad_down_ref[cut, :] = matmul(hidden_t[cut, :], y_all[:, columns]).astype(jnp.bfloat16)
+        return carry
+
+    lax.fori_loop(0, units // BLOCK, all_backward, 0)
+
+    slot_column = jnp.sum(jnp.where(diagonal, slot, 0), axis=1, keepdims=True)
+    combine = (
+        lax.broadcasted_iota(jnp.int32, (tok, out_back.shape[0]), 1) == slot_column
+    ).astype(jnp.bfloat16)
+    for s in steps:
+        back(0, s).wait_recv()
+    expert_out = matmul(combine, out_back[...])
+    out_ref[...] = (prob * expert_out).astype(jnp.bfloat16)
+    d_gate = jnp.sum(expert_out * cot_ref[...].astype(jnp.float32), axis=1, keepdims=True)
+    d_gate_ref[...] = jnp.sum(jnp.where(diagonal, d_gate, 0.0), axis=0, keepdims=True)
+    for s in steps:
+        back(1, s).wait_recv()
+    dx_ref[...] = matmul(combine, dx_back[...]).astype(jnp.bfloat16)
+
+    for array in range(2):
+        for s in steps:
+            go(array, s).wait_send()
+            back(array, s).wait_send()
+        for kind in range(3):
+            for s in range(n):
+                forward(array, s, kind).wait_send()
+
+
+def fused(n, tokens, expert_choice, gate_prob, cotangent, w_gate, w_up, w_down):
+    tok, features = tokens.shape
+    units = w_gate.shape[1]
+    capacity = 3 * tok // (2 * n)
+    own = n * capacity
+    everyone = 4 * own
+    padded = -(-own // LANES) * LANES
+    width = features // 4
+    bf16, f32 = jnp.bfloat16, jnp.float32
+    vmem = pl.BlockSpec(memory_space=pltpu.VMEM)
+    hbm = pl.BlockSpec(memory_space=pl.ANY)
+    work = 2 * units * features * (6 * own + 3 * everyone + 3 * own)
+    layer_out, d_tokens, d_gate, *grads = pl.pallas_call(
+        functools.partial(kernel, n, capacity),
+        out_shape=(
+            jax.ShapeDtypeStruct((tok, features), bf16),
+            jax.ShapeDtypeStruct((tok, features), bf16),
+            jax.ShapeDtypeStruct((1, tok), f32),
+        )
+        + (jax.ShapeDtypeStruct((units, width), bf16),) * 3,
+        in_specs=[vmem] * 4 + [hbm] * 3,
+        out_specs=(vmem,) * 6,
+        scratch_shapes=[
+            pltpu.VMEM((units, features), bf16),
+            pltpu.VMEM((units, features), bf16),
+            pltpu.VMEM((units, features), bf16),
+            pltpu.VMEM((own - capacity, features), bf16),
+            pltpu.VMEM((own - capacity, features), bf16),
+            pltpu.VMEM((everyone, features), bf16),
+            pltpu.VMEM((everyone, features), bf16),
+            pltpu.VMEM((own, units), f32),
+            pltpu.VMEM((own, units), f32),
+            pltpu.VMEM((own, units), bf16),
+            pltpu.VMEM((own, units), bf16),
+            pltpu.VMEM((own, units), bf16),
+            pltpu.VMEM((units, everyone), f32),
+            pltpu.VMEM((units, everyone), f32),
+            pltpu.VMEM((units, everyone), bf16),
+            pltpu.VMEM((own, features), bf16),
+            pltpu.VMEM((own, features), bf16),
+            pltpu.VMEM((padded, features), bf16),
+            pltpu.VMEM((padded, features), bf16),
+            pltpu.SemaphoreType.DMA((3,)),
+            pltpu.SemaphoreType.DMA((2, n)),
+            pltpu.SemaphoreType.DMA((2, n)),
+            pltpu.SemaphoreType.DMA((2, 3, n)),
+            pltpu.SemaphoreType.DMA((2, 3, n)),
+            pltpu.SemaphoreType.DMA((2, n)),
+            pltpu.SemaphoreType.DMA((2, n)),
+        ],
+        cost_estimate=pl.CostEstimate(
+            flops=work, bytes_accessed=6 * units * features, transcendentals=units * everyone
+        ),
+        compiler_params=pltpu.CompilerParams(
+            collective_id=0, has_side_effects=True, vmem_limit_bytes=40 * 1024 * 1024
+        ),
+    )(
+        tokens,
+        expert_choice.reshape(1, tok),
+        gate_prob.reshape(1, tok),
+        cotangent,
+        w_gate[0],
+        w_up[0],
+        w_down[0],
+    )
+    return (layer_out, d_tokens, d_gate.reshape(tok, 1), *(grad[None] for grad in grads))
+
+
 def solution(mesh):
     in_specs = (
         P(("parts", "expert", "dp", "sub"), None),
@@ -125,4 +449,14 @@
         P(("parts", "expert"), "sub", "dp"),
         P(("parts", "expert"), "sub", "dp"),
     )
-    return jax.shard_map(local, mesh=mesh, in_specs=in_specs, out_specs=out_specs, check_vma=False)
+    shape = dict(mesh.shape)
+    fits = shape["sub"] == 1 and shape["dp"] == 4
+
+    def device_part(tokens, expert_choice, *rest):
+        capacity = 3 * tokens.shape[0] // (2 * shape["expert"])
+        one_choice = expert_choice.shape[1] == 1
+        if fits and one_choice and tokens.shape[0] == LANES and capacity % 16 == 0:
+            return fused(shape["expert"], tokens, expert_choice, *rest)
+        return local(tokens, expert_choice, *rest)
+
+    return jax.shard_map(device_part, mesh=mesh, in_specs=in_specs, out_specs=out_specs, check_vma=False)

time: 148 us -> 57.1 us (0.39)
  waiting for transfers between devices: 85.4 us -> 0 us
  Pallas kernels: 0 us -> 44.6 us
  matrix products: 25.8 us -> 0 us
  starting transfers between devices: 17.6 us -> 0 us
  between operations: 13.9 us -> 0.66 us
  local copies, waits for them, and re-layouts: 2.58 us -> 11.6 us
  other arithmetic: 2.53 us -> 0 us
    reduce_scatter x3 -> x0, waiting for transfers between devices: 50.2 us -> none  [the longest x1 31.3 us: local(): lax.psum_scatter(grad_down.astype(jnp.bfloat16), 'dp', scatter_dimension=...]
    pallas_call x0 -> x1, Pallas kernels: none -> 44.6 us  [fused(): pl.pallas_call(functools.partial(kernel, n, capacity), out_shape=(jax.Sha...]
    all_to_all x4 -> x0, waiting for transfers between devices: 35.1 us -> none  [the longest x1 10.6 us: local(): lax.all_to_all(x_send, 'expert', split_axis=0, concat_axis=0, tiled=True)]
    dot_general x13 -> x0, matrix products: 25.8 us -> none  [the longest x5 10.9 us: contract_rows(): lax.dot_general(left, right, (((0,), (0,)), ((), ())), preferred_element_...]
    all_to_all x4 -> x0, starting transfers between devices: 17.5 us -> none  [the longest x1 6.32 us: local(): lax.all_to_all(x_send, 'expert', split_axis=0, concat_axis=0, tiled=True)]
    unnamed x18 -> x20, local copies, waits for them, and re-layouts: 2.58 us -> 11.6 us
  transfers between devices with their start and end apart: 7 -> 0, of which waited for: 6 -> 0; matrix products, arithmetic and copies ran while one was open for 13% -> 0% of each run, Pallas kernels for 0% -> 0%
where the time goes in v1:
time: 57.1 us; the launch traced here: 56.8 us
  Pallas kernels  44.6 us (78%)
  local copies, waits for them, and re-layouts  11.6 us (20%)
  between operations  0.66 us (1%)
    pallas_call x1, Pallas kernels, fused(): pl.pallas_call(functools.partial(kernel, n, capacity), out_shape=(jax.Sha...  44.6 us
    unnamed x20, local copies, waits for them, and re-layouts  11.6 us

profile of v1, /device:TPU:0, one launch (start us, length us, event | category | flops | bytes accessed | tf_op | source)
XLA Modules:
  0.0 56.8 jit_solution(4136290182135472255)
XLA Ops:
  0.6 0.0 copy-start
  0.6 1.4 %copy-done = bf16[1,768,1024]{2,1,0:T(8,128)(2,1)S(1)} copy-done((bf16[1,768,1024]{2,1,0:T(8,128)(2,1)S(1)}, bf16[1,768,1024]{2,1,0:T(8,128)(2,1)}, u32[]{:S(2)}) %copy-start) | copy-done | bytes 1572888
  2.0 0.0 copy-start.1
  2.0 1.4 %copy-done.1 = bf16[1,768,1024]{2,1,0:T(8,128)(2,1)S(1)} copy-done((bf16[1,768,1024]{2,1,0:T(8,128)(2,1)S(1)}, bf16[1,768,1024]{2,1,0:T(8,128)(2,1)}, u32[]{:S(2)}) %copy-start.1) | copy-done | bytes 1572888
  3.5 0.0 copy-start.2
  3.5 1.4 %copy-done.2 = bf16[1,768,1024]{2,1,0:T(8,128)(2,1)S(1)} copy-done((bf16[1,768,1024]{2,1,0:T(8,128)(2,1)S(1)}, bf16[1,768,1024]{2,1,0:T(8,128)(2,1)}, u32[]{:S(2)}) %copy-start.2) | copy-done | bytes 1572888
  4.9 0.0 copy-start.3
  4.9 0.9 %copy-done.3 = bf16[128,1024]{1,0:T(8,128)(2,1)S(1)} copy-done((bf16[128,1024]{1,0:T(8,128)(2,1)S(1)}, bf16[128,1024]{1,0:T(8,128)(2,1)}, u32[]{:S(2)}) %copy-start.3) | copy-done | bytes 262168
  5.8 0.0 copy-start.4
  5.8 0.9 %copy-done.4 = bf16[128,1024]{1,0:T(8,128)(2,1)S(1)} copy-done((bf16[128,1024]{1,0:T(8,128)(2,1)S(1)}, bf16[128,1024]{1,0:T(8,128)(2,1)}, u32[]{:S(2)}) %copy-start.4) | copy-done | bytes 262168
  6.8 0.0 copy-start.5
  6.8 0.7 %copy-done.5 = s32[128,1]{0,1:T(1,128)S(1)} copy-done((s32[128,1]{0,1:T(1,128)S(1)}, s32[128,1]{0,1:T(1,128)}, u32[]{:S(2)}) %copy-start.5) | copy-done | bytes 536
  7.4 0.0 copy-start.6
  7.4 0.7 %copy-done.6 = f32[128,1]{0,1:T(1,128)S(1)} copy-done((f32[128,1]{0,1:T(1,128)S(1)}, f32[128,1]{0,1:T(1,128)}, u32[]{:S(2)}) %copy-start.6) | copy-done | bytes 536
  8.1 44.6 %shard_map.118 = (bf16[128,1024]{1,0:T(8,128)(2,1)S(1)}, bf16[128,1024]{1,0:T(8,128)(2,1)S(1)}, f32[1,128]{1,0:T(1,128)S(1)}, bf16[768,256]{1,0:T(8,128)(2,1)S(1...) custom-call(bf16[128,1024]{1,0:T(8,128)(2,1)S(1)} %copy-done.3, s32[1,128]{1,0:T(1,128)S(1)} %bitcast.15, ...), custom_call_target="tpu_custom_call" | custom-call | flops 6341787648 | bytes 4718592 | tf_op jit(solution)/shard_map/pallas_call | solution.py:378
  52.6 0.7 %copy.19 = bf16[128,1024]{1,0:T(8,128)(2,1)} copy(bf16[128,1024]{1,0:T(8,128)(2,1)S(1)} %get-tuple-element.24) | data formatting | bytes 524288
  53.4 0.7 %copy.20 = bf16[128,1024]{1,0:T(8,128)(2,1)} copy(bf16[128,1024]{1,0:T(8,128)(2,1)S(1)} %get-tuple-element.25) | data formatting | bytes 524288
  54.1 0.5 copy.21
  54.6 0.7 %copy.22 = bf16[1,768,256]{2,1,0:T(8,128)(2,1)} copy(bf16[1,768,256]{2,1,0:T(8,128)(2,1)S(1)} %bitcast.11) | data formatting | bytes 786432
  55.3 0.7 %copy.23 = bf16[1,768,256]{2,1,0:T(8,128)(2,1)} copy(bf16[1,768,256]{2,1,0:T(8,128)(2,1)S(1)} %bitcast.10) | data formatting | bytes 786432
  56.1 0.7 %copy.24 = bf16[1,768,256]{2,1,0:T(8,128)(2,1)} copy(bf16[1,768,256]{2,1,0:T(8,128)(2,1)S(1)} %bitcast.9) | data formatting | bytes 786432
Async XLA Ops:
  0.6 1.4 %copy-start = (bf16[1,768,1024]{2,1,0:T(8,128)(2,1)S(1)}, bf16[1,768,1024]{2,1,0:T(8,128)(2,1)}, u32[]{:S(2)}) copy-start(bf16[1,768,1024]{2,1,0:T(8,128)(2,1)} %param.11) | copy-start | bytes 4718596
  2.0 1.4 %copy-start.1 = (bf16[1,768,1024]{2,1,0:T(8,128)(2,1)S(1)}, bf16[1,768,1024]{2,1,0:T(8,128)(2,1)}, u32[]{:S(2)}) copy-start(bf16[1,768,1024]{2,1,0:T(8,128)(2,1)} %param.12) | copy-start | bytes 4718596
  3.5 1.4 %copy-start.2 = (bf16[1,768,1024]{2,1,0:T(8,128)(2,1)S(1)}, bf16[1,768,1024]{2,1,0:T(8,128)(2,1)}, u32[]{:S(2)}) copy-start(bf16[1,768,1024]{2,1,0:T(8,128)(2,1)} %param.13) | copy-start | bytes 4718596
  4.9 0.9 %copy-start.3 = (bf16[128,1024]{1,0:T(8,128)(2,1)S(1)}, bf16[128,1024]{1,0:T(8,128)(2,1)}, u32[]{:S(2)}) copy-start(bf16[128,1024]{1,0:T(8,128)(2,1)} %tokens_ref.1) | copy-start | bytes 786436
  5.8 0.9 %copy-start.4 = (bf16[128,1024]{1,0:T(8,128)(2,1)S(1)}, bf16[128,1024]{1,0:T(8,128)(2,1)}, u32[]{:S(2)}) copy-start(bf16[128,1024]{1,0:T(8,128)(2,1)} %cot_ref.1) | copy-start | bytes 786436
  6.8 0.7 %copy-start.5 = (s32[128,1]{0,1:T(1,128)S(1)}, s32[128,1]{0,1:T(1,128)}, u32[]{:S(2)}) copy-start(s32[128,1]{0,1:T(1,128)} %param.8) | copy-start | bytes 1540
  7.4 0.7 %copy-start.6 = (f32[128,1]{0,1:T(1,128)S(1)}, f32[128,1]{0,1:T(1,128)}, u32[]{:S(2)}) copy-start(f32[128,1]{0,1:T(1,128)} %param.9) | copy-start | bytes 1540

commit v2 on v1

--- a/solution.py
+++ b/solution.py
@@ -122,13 +122,44 @@
 
 def kernel(
     n, capacity,
-    tokens_ref, choice_ref, prob_ref, cot_ref, w_gate_hbm, w_up_hbm, w_down_hbm,
-    out_ref, dx_ref, d_gate_ref, grad_gate_ref, grad_up_ref, grad_down_ref,
+    tokens_hbm, choice_hbm, prob_hbm, cot_hbm, w_gate_hbm, w_up_hbm, w_down_hbm,
+    out_hbm, dx_hbm, d_gate_hbm, grad_gate_hbm, grad_up_hbm, grad_down_hbm,
+    tokens_ref, choice_ref, prob_ref, cot_ref,
     w_gate, w_up, w_down, x_send, y_send, x_all, y_all,
     active, slope, hidden, d_gate_pre, d_up_pre,
     active_t, slope_t, hidden_t, out_rows, dx_rows, out_back, dx_back,
-    load_sem, go_sem, go_recv, fwd_sem, fwd_recv, back_sem, back_recv,
+    out_ref, dx_ref, d_gate_ref, grad_gate_ref, grad_up_ref, grad_down_ref,
+    load_sem, store_sem, go_sem, go_recv, fwd_sem, fwd_recv, back_sem, back_recv,
 ):
+    loads = [
+        pltpu.make_async_copy(src, dst, load_sem.at[i])
+        for i, (src, dst) in enumerate(
+            (
+                (choice_hbm, choice_ref),
+                (tokens_hbm, tokens_ref),
+                (prob_hbm, prob_ref),
+                (cot_hbm, cot_ref),
+                (w_gate_hbm, w_gate),
+                (w_up_hbm, w_up),
+                (w_down_hbm, w_down),
+            )
+        )
+    ]
+    for load in loads:
+        load.start()
+    stores = [
+        pltpu.make_async_copy(src, dst, store_sem.at[i])
+        for i, (src, dst) in enumerate(
+            (
+                (out_ref, out_hbm),
+                (dx_ref, dx_hbm),
+                (d_gate_ref, d_gate_hbm),
+                (grad_gate_ref, grad_gate_hbm),
+                (grad_up_ref, grad_up_hbm),
+                (grad_down_ref, grad_down_hbm),
+            )
+        )
+    ]
     me = lax.axis_index("expert")
     dp = lax.axis_index("dp")
     sibling = dp + 1 - 2 * lax.rem(dp, 2)
@@ -146,15 +177,7 @@
     for d in (sibling, across):
         pl.semaphore_signal(barrier, inc=1, device_id={"dp": d}, device_id_type=MESH)
 
-    loads = [
-        pltpu.make_async_copy(src, dst, load_sem.at[i])
-        for i, (src, dst) in enumerate(
-            ((w_gate_hbm, w_gate), (w_up_hbm, w_up), (w_down_hbm, w_down))
-        )
-    ]
-    for load in loads:
-        load.start()
-
+    loads[0].wait()
     choice = choice_ref[...]
     relative = choice - me
     relative = jnp.where(relative < 0, relative + n, relative)
@@ -171,7 +194,6 @@
         lax.broadcasted_iota(jnp.int32, (own, tok), 0) == slot
     ).astype(jnp.bfloat16)
     diagonal = row_id == col_id
-    prob = jnp.sum(jnp.where(diagonal, prob_ref[...], 0.0), axis=1, keepdims=True)
 
     def rows(s, group=0):
         return pl.ds(group * own + s * capacity, capacity)
@@ -215,12 +237,16 @@
             device_id_type=MESH,
         )
 
+    loads[1].wait()
     dispatch(tokens_ref[...], x_send, x_all, 0)
     pl.semaphore_wait(barrier, n + 1)
     for s in steps:
         go(0, s).start()
     forward(0, 0, 1).start()
     forward(0, 0, 0).start()
+    loads[2].wait()
+    loads[3].wait()
+    prob = jnp.sum(jnp.where(diagonal, prob_ref[...], 0.0), axis=1, keepdims=True)
     scaled = (prob * cot_ref[...].astype(jnp.float32)).astype(jnp.bfloat16)
     dispatch(scaled, y_send, y_all, 1)
     for s in steps:
@@ -232,7 +258,7 @@
     if tail:
         out_back[pl.ds(own, tail), :] = jnp.zeros((tail, features), jnp.bfloat16)
         dx_back[pl.ds(own, tail), :] = jnp.zeros((tail, features), jnp.bfloat16)
-    for load in loads:
+    for load in loads[4:]:
         load.wait()
 
     for s in steps:
@@ -340,6 +366,8 @@
 
     lax.fori_loop(0, units // BLOCK, all_backward, 0)
 
+    for store in stores[3:]:
+        store.start()
     slot_column = jnp.sum(jnp.where(diagonal, slot, 0), axis=1, keepdims=True)
     combine = (
         lax.broadcasted_iota(jnp.int32, (tok, out_back.shape[0]), 1) == slot_column
@@ -350,9 +378,12 @@
     out_ref[...] = (prob * expert_out).astype(jnp.bfloat16)
     d_gate = jnp.sum(expert_out * cot_ref[...].astype(jnp.float32), axis=1, keepdims=True)
     d_gate_ref[...] = jnp.sum(jnp.where(diagonal, d_gate, 0.0), axis=0, keepdims=True)
+    stores[0].start()
+    stores[2].start()
     for s in steps:
         back(1, s).wait_recv()
     dx_ref[...] = matmul(combine, dx_back[...]).astype(jnp.bfloat16)
+    stores[1].start()
 
     for array in range(2):
         for s in steps:
@@ -361,6 +392,20 @@
         for kind in range(3):
             for s in range(n):
                 forward(array, s, kind).wait_send()
+    for store in stores:
+        store.wait()
+
+
+def write_out(*refs):
+    made, results, sem = refs[:6], refs[6:12], refs[12]
+    copies = [
+        pltpu.make_async_copy(src, dst, sem.at[i])
+        for i, (src, dst) in enumerate(zip(made, results))
+    ]
+    for copy in copies:
+        copy.start()
+    for copy in copies:
+        copy.wait()
 
 
 def fused(n, tokens, expert_choice, gate_prob, cotangent, w_gate, w_up, w_down):
@@ -372,10 +417,9 @@
     padded = -(-own // LANES) * LANES
     width = features // 4
     bf16, f32 = jnp.bfloat16, jnp.float32
-    vmem = pl.BlockSpec(memory_space=pltpu.VMEM)
-    hbm = pl.BlockSpec(memory_space=pl.ANY)
+    hbm = pl.BlockSpec(memory_space=pltpu.HBM)
     work = 2 * units * features * (6 * own + 3 * everyone + 3 * own)
-    layer_out, d_tokens, d_gate, *grads = pl.pallas_call(
+    results = pl.pallas_call(
         functools.partial(kernel, n, capacity),
         out_shape=(
             jax.ShapeDtypeStruct((tok, features), bf16),
@@ -383,9 +427,13 @@
             jax.ShapeDtypeStruct((1, tok), f32),
         )
         + (jax.ShapeDtypeStruct((units, width), bf16),) * 3,
-        in_specs=[vmem] * 4 + [hbm] * 3,
-        out_specs=(vmem,) * 6,
+        in_specs=[hbm] * 7,
+        out_specs=(hbm,) * 6,
         scratch_shapes=[
+            pltpu.VMEM((tok, features), bf16),
+            pltpu.VMEM((1, tok), jnp.int32),
+            pltpu.VMEM((1, tok), f32),
+            pltpu.VMEM((tok, features), bf16),
             pltpu.VMEM((units, features), bf16),
             pltpu.VMEM((units, features), bf16),
             pltpu.VMEM((units, features), bf16),
@@ -405,7 +453,14 @@
             pltpu.VMEM((own, features), bf16),
             pltpu.VMEM((padded, features), bf16),
             pltpu.VMEM((padded, features), bf16),
-            pltpu.SemaphoreType.DMA((3,)),
+            pltpu.VMEM((tok, features), bf16),
+            pltpu.VMEM((tok, features), bf16),
+            pltpu.VMEM((1, tok), f32),
+            pltpu.VMEM((units, width), bf16),
+            pltpu.VMEM((units, width), bf16),
+            pltpu.VMEM((units, width), bf16),
+            pltpu.SemaphoreType.DMA((7,)),
+            pltpu.SemaphoreType.DMA((6,)),
             pltpu.SemaphoreType.DMA((2, n)),
             pltpu.SemaphoreType.DMA((2, n)),
             pltpu.SemaphoreType.DMA((2, 3, n)),
@@ -417,7 +472,7 @@
             flops=work, bytes_accessed=6 * units * features, transcendentals=units * everyone
         ),
         compiler_params=pltpu.CompilerParams(
-            collective_id=0, has_side_effects=True, vmem_limit_bytes=40 * 1024 * 1024
+            collective_id=0, has_side_effects=True, vmem_limit_bytes=60 * 1024 * 1024
         ),
     )(
         tokens,
@@ -428,6 +483,14 @@
         w_up[0],
         w_down[0],
     )
+    layer_out, d_tokens, d_gate, *grads = pl.pallas_call(
+        write_out,
+        out_shape=tuple(jax.ShapeDtypeStruct(r.shape, r.dtype) for r in results),
+        in_specs=[hbm] * 6,
+        out_specs=(hbm,) * 6,
+        scratch_shapes=[pltpu.SemaphoreType.DMA((6,))],
+        compiler_params=pltpu.CompilerParams(vmem_limit_bytes=60 * 1024 * 1024),
+    )(*results)
     return (layer_out, d_tokens, d_gate.reshape(tok, 1), *(grad[None] for grad in grads))
 
 

time: 57.1 us -> 98.9 us (1.73)
  Pallas kernels: 44.6 us -> 98.1 us
  local copies, waits for them, and re-layouts: 11.6 us -> 0 us
    pallas_call x0 -> x1, Pallas kernels: none -> 52.8 us  [fused(): pl.pallas_call(write_out, out_shape=tuple((jax.ShapeDtypeStruct(r.shape,...]
    unnamed x20 -> x0, local copies, waits for them, and re-layouts: 11.6 us -> none
where the time goes in v2:
time: 98.9 us; the launch traced here: 98.8 us
  Pallas kernels  98.1 us (99%)
    pallas_call x1, Pallas kernels, fused(): pl.pallas_call(write_out, out_shape=tuple((jax.ShapeDtypeStruct(r.shape,...  52.8 us
    pallas_call x1, Pallas kernels, fused(): pl.pallas_call(functools.partial(kernel, n, capacity), out_shape=(jax.Sha...  45.3 us

profile of v2, /device:TPU:0, one launch (start us, length us, event | category | flops | bytes accessed | tf_op | source)
XLA Modules:
  0.0 98.8 jit_solution(13802603324152991906)
XLA Ops:
  0.6 45.3 %shard_map.118 = (bf16[128,1024]{1,0:T(8,128)(2,1)}, bf16[128,1024]{1,0:T(8,128)(2,1)}, f32[1,128]{1,0:T(1,128)}, bf16[768,256]{1,0:T(8,128)(2,1)}, bf16[768,256]{1,0:T(8,128)(2,1)}, /*index=5*/bf16[768,256]{1,0:T(8,128)(2,1)}) custom-call(bf16[128,1024]{1,0:T(8,128)(2,1)} %tokens_hbm.1, s32[1,128]{1,0:T(1,128)} %bitcast.15, f32[1,128]{1,0:T(1,128)} %bitcast.16, ...), custom_call_target="tpu_custom_call" | custom-call | flops 6341787648 | bytes 4718592 | tf_op jit(solution)/shard_map/pallas_call | solution.py:422
  46.0 52.8 %shard_map.119 = (bf16[128,1024]{1,0:T(8,128)(2,1)}, bf16[128,1024]{1,0:T(8,128)(2,1)}, f32[1,128]{1,0:T(1,128)}, bf16[768,256]{1,0:T(8,128)(2,1)}, bf16[768,256]{1,0:T(8,128)(2,1)}, /*index=5*/bf16[768,256]{1,0:T(8,128)(2,1)}) custom-call(bf16[128,1024]{1,0:T(8,128)(2,1)} %get-tuple-element.18.refs_0_, bf16[128,1024]{1,0:T(8,128)(2,1)} %get-tuple-element.19.refs_1_, ...), custom_call_target="tpu_custom_call" | custom-call | tf_op jit(solution)/shard_map/pallas_call | solution.py:486

commit v3 on v2

--- a/solution.py
+++ b/solution.py
@@ -397,15 +397,22 @@
 
 
 def write_out(*refs):
-    made, results, sem = refs[:6], refs[6:12], refs[12]
-    copies = [
-        pltpu.make_async_copy(src, dst, sem.at[i])
-        for i, (src, dst) in enumerate(zip(made, results))
+    made, results, held, sem = refs[:6], refs[6:12], refs[12:18], refs[18]
+    reads = [
+        pltpu.make_async_copy(src, dst, sem.at[0, i])
+        for i, (src, dst) in enumerate(zip(made, held))
     ]
-    for copy in copies:
-        copy.start()
-    for copy in copies:
-        copy.wait()
+    writes = [
+        pltpu.make_async_copy(src, dst, sem.at[1, i])
+        for i, (src, dst) in enumerate(zip(held, results))
+    ]
+    for read in reads:
+        read.start()
+    for read, write in zip(reads, writes):
+        read.wait()
+        write.start()
+    for write in writes:
+        write.wait()
 
 
 def fused(n, tokens, expert_choice, gate_prob, cotangent, w_gate, w_up, w_down):
@@ -488,7 +495,8 @@
         out_shape=tuple(jax.ShapeDtypeStruct(r.shape, r.dtype) for r in results),
         in_specs=[hbm] * 6,
         out_specs=(hbm,) * 6,
-        scratch_shapes=[pltpu.SemaphoreType.DMA((6,))],
+        scratch_shapes=[pltpu.VMEM(r.shape, r.dtype) for r in results]
+        + [pltpu.SemaphoreType.DMA((2, 6))],
         compiler_params=pltpu.CompilerParams(vmem_limit_bytes=60 * 1024 * 1024),
     )(*results)
     return (layer_out, d_tokens, d_gate.reshape(tok, 1), *(grad[None] for grad in grads))

time: 98.9 us -> 48.4 us (0.49)
  Pallas kernels: 98.1 us -> 47.6 us
    pallas_call x1, Pallas kernels: 52.8 us -> 2.27 us  [fused(): pl.pallas_call(write_out, out_shape=tuple((jax.ShapeDtypeStruct(r.shape,...]
where the time goes in v3:
time: 48.4 us; the launch traced here: 48.2 us
  Pallas kernels  47.6 us (98%)
  between operations  0.64 us (1%)
    pallas_call x1, Pallas kernels, fused(): pl.pallas_call(functools.partial(kernel, n, capacity), out_shape=(jax.Sha...  45.3 us
    pallas_call x1, Pallas kernels, fused(): pl.pallas_call(write_out, out_shape=tuple((jax.ShapeDtypeStruct(r.shape,...  2.27 us

profile of v3, /device:TPU:0, one launch (start us, length us, event | category | flops | bytes accessed | tf_op | source)
XLA Modules:
  0.0 48.2 jit_solution(11332366070646015169)
XLA Ops:
  0.6 45.3 %shard_map.118 = (bf16[128,1024]{1,0:T(8,128)(2,1)}, bf16[128,1024]{1,0:T(8,128)(2,1)}, f32[1,128]{1,0:T(1,128)}, bf16[768,256]{1,0:T(8,128)(2,1)}, bf16[768,256]{1,0:T(8,128)(2,1)}, /*index=5*/bf16[768,256]{1,0:T(8,128)(2,1)}) custom-call(bf16[128,1024]{1,0:T(8,128)(2,1)} %tokens_hbm.1, s32[1,128]{1,0:T(1,128)} %bitcast.15, f32[1,128]{1,0:T(1,128)} %bitcast.16, ...), custom_call_target="tpu_custom_call" | custom-call | flops 6341787648 | bytes 4718592 | tf_op jit(solution)/shard_map/pallas_call | solution.py:429
  46.0 2.3 %shard_map.119 = (bf16[128,1024]{1,0:T(8,128)(2,1)}, bf16[128,1024]{1,0:T(8,128)(2,1)}, f32[1,128]{1,0:T(1,128)}, bf16[768,256]{1,0:T(8,128)(2,1)}, bf16[768,256]{1,0:T(8,128)(2,1)}, /*index=5*/bf16[768,256]{1,0:T(8,128)(2,1)}) custom-call(bf16[128,1024]{1,0:T(8,128)(2,1)} %get-tuple-element.18.refs_0_, bf16[128,1024]{1,0:T(8,128)(2,1)} %get-tuple-element.19.refs_1_, ...), custom_call_target="tpu_custom_call" | custom-call | tf_op jit(solution)/shard_map/pallas_call | solution.py:493

commit v4 on v3

--- a/solution.py
+++ b/solution.py
@@ -169,7 +169,7 @@
     own = n * capacity
     units = w_gate.shape[0]
     features = w_gate.shape[1]
-    steps = range(1, n)
+    steps = range(n - 1, 0, -1)
 
     barrier = pltpu.get_barrier_semaphore()
     for s in steps:
@@ -315,7 +315,7 @@
         hidden_t[cut, :] = made
         return carry
 
-    lax.fori_loop(0, units // BLOCK, all_forward, 0)
+    lax.fori_loop(0, units // BLOCK - 1, all_forward, 0)
 
     for s in steps:
         go(1, s).wait_recv()
@@ -342,6 +342,7 @@
     for s in steps:
         back(1, s).start()
     dx_back[pl.ds(0, capacity), :] = dx_rows[pl.ds(0, capacity), :]
+    lax.fori_loop(units // BLOCK - 1, units // BLOCK, all_forward, 0)
 
     for s in range(n):
         forward(1, s, 1).wait_recv()

time: 48.4 us -> 47.4 us (0.979)
  Pallas kernels: 47.6 us -> 46.6 us
    pallas_call x1, Pallas kernels: 45.3 us -> 44.3 us  [fused(): pl.pallas_call(functools.partial(kernel, n, capacity), out_shape=(jax.Sha...]
where the time goes in v4:
time: 47.4 us; the launch traced here: 47.2 us
  Pallas kernels  46.6 us (98%)
  between operations  0.64 us (1%)
    pallas_call x1, Pallas kernels, fused(): pl.pallas_call(functools.partial(kernel, n, capacity), out_shape=(jax.Sha...  44.3 us
    pallas_call x1, Pallas kernels, fused(): pl.pallas_call(write_out, out_shape=tuple((jax.ShapeDtypeStruct(r.shape,...  2.27 us

profile of v4, /device:TPU:0, one launch (start us, length us, event | category | flops | bytes accessed | tf_op | source)
XLA Modules:
  0.0 47.2 jit_solution(9761905232325731641)
XLA Ops:
  0.6 44.3 %shard_map.118 = (bf16[128,1024]{1,0:T(8,128)(2,1)}, bf16[128,1024]{1,0:T(8,128)(2,1)}, f32[1,128]{1,0:T(1,128)}, bf16[768,256]{1,0:T(8,128)(2,1)}, bf16[768,256]{1,0:T(8,128)(2,1)}, /*index=5*/bf16[768,256]{1,0:T(8,128)(2,1)}) custom-call(bf16[128,1024]{1,0:T(8,128)(2,1)} %tokens_hbm.1, s32[1,128]{1,0:T(1,128)} %bitcast.15, f32[1,128]{1,0:T(1,128)} %bitcast.16, ...), custom_call_target="tpu_custom_call" | custom-call | flops 6341787648 | bytes 4718592 | tf_op jit(solution)/shard_map/pallas_call | solution.py:430
  44.9 2.3 %shard_map.119 = (bf16[128,1024]{1,0:T(8,128)(2,1)}, bf16[128,1024]{1,0:T(8,128)(2,1)}, f32[1,128]{1,0:T(1,128)}, bf16[768,256]{1,0:T(8,128)(2,1)}, bf16[768,256]{1,0:T(8,128)(2,1)}, /*index=5*/bf16[768,256]{1,0:T(8,128)(2,1)}) custom-call(bf16[128,1024]{1,0:T(8,128)(2,1)} %get-tuple-element.18.refs_0_, bf16[128,1024]{1,0:T(8,128)(2,1)} %get-tuple-element.19.refs_1_, ...), custom_call_target="tpu_custom_call" | custom-call | tf_op jit(solution)/shard_map/pallas_call | solution.py:494

commit v5 on v4

--- a/solution.py
+++ b/solution.py
@@ -123,12 +123,12 @@
 def kernel(
     n, capacity,
     tokens_hbm, choice_hbm, prob_hbm, cot_hbm, w_gate_hbm, w_up_hbm, w_down_hbm,
-    out_hbm, dx_hbm, d_gate_hbm, grad_gate_hbm, grad_up_hbm, grad_down_hbm,
+    out_hbm, dx_back, combine_hbm, d_gate_hbm, grad_gate_hbm, grad_up_hbm, grad_down_hbm,
     tokens_ref, choice_ref, prob_ref, cot_ref,
     w_gate, w_up, w_down, x_send, y_send, x_all, y_all,
     active, slope, hidden, d_gate_pre, d_up_pre,
-    active_t, slope_t, hidden_t, out_rows, dx_rows, out_back, dx_back,
-    out_ref, dx_ref, d_gate_ref, grad_gate_ref, grad_up_ref, grad_down_ref,
+    active_t, slope_t, hidden_t, out_rows, dx_rows, out_back,
+    out_ref, combine_ref, d_gate_ref, grad_gate_ref, grad_up_ref, grad_down_ref,
     load_sem, store_sem, go_sem, go_recv, fwd_sem, fwd_recv, back_sem, back_recv,
 ):
     loads = [
@@ -152,11 +152,12 @@
         for i, (src, dst) in enumerate(
             (
                 (out_ref, out_hbm),
-                (dx_ref, dx_hbm),
+                (combine_ref, combine_hbm),
                 (d_gate_ref, d_gate_hbm),
                 (grad_gate_ref, grad_gate_hbm),
                 (grad_up_ref, grad_up_hbm),
                 (grad_down_ref, grad_down_hbm),
+                (dx_rows.at[pl.ds(0, capacity)], dx_back.at[pl.ds(0, capacity)]),
             )
         )
     ]
@@ -257,7 +258,6 @@
     tail = out_back.shape[0] - own
     if tail:
         out_back[pl.ds(own, tail), :] = jnp.zeros((tail, features), jnp.bfloat16)
-        dx_back[pl.ds(own, tail), :] = jnp.zeros((tail, features), jnp.bfloat16)
     for load in loads[4:]:
         load.wait()
 
@@ -341,7 +341,7 @@
     lax.fori_loop(0, features // BLOCK, own_dx, 0)
     for s in steps:
         back(1, s).start()
-    dx_back[pl.ds(0, capacity), :] = dx_rows[pl.ds(0, capacity), :]
+    stores[6].start()
     lax.fori_loop(units // BLOCK - 1, units // BLOCK, all_forward, 0)
 
     for s in range(n):
@@ -367,12 +367,14 @@
 
     lax.fori_loop(0, units // BLOCK, all_backward, 0)
 
-    for store in stores[3:]:
+    for store in stores[3:6]:
         store.start()
     slot_column = jnp.sum(jnp.where(diagonal, slot, 0), axis=1, keepdims=True)
     combine = (
         lax.broadcasted_iota(jnp.int32, (tok, out_back.shape[0]), 1) == slot_column
     ).astype(jnp.bfloat16)
+    combine_ref[...] = combine
+    stores[1].start()
     for s in steps:
         back(0, s).wait_recv()
     expert_out = matmul(combine, out_back[...])
@@ -383,8 +385,6 @@
     stores[2].start()
     for s in steps:
         back(1, s).wait_recv()
-    dx_ref[...] = matmul(combine, dx_back[...]).astype(jnp.bfloat16)
-    stores[1].start()
 
     for array in range(2):
         for s in steps:
@@ -398,18 +398,29 @@
 
 
 def write_out(*refs):
-    made, results, held, sem = refs[:6], refs[6:12], refs[12:18], refs[18]
+    made, results, held, dx_ref, sem = refs[:7], refs[7:13], refs[13:20], refs[20], refs[21]
+    dx_held, combine_held = held[:2]
+    own = made[0].shape[0]
+    tail = dx_held.shape[0] - own
+    landing = (dx_held.at[pl.ds(0, own)],) + tuple(held[1:])
     reads = [
         pltpu.make_async_copy(src, dst, sem.at[0, i])
-        for i, (src, dst) in enumerate(zip(made, held))
+        for i, (src, dst) in enumerate(zip(made, landing))
     ]
+    sources = (dx_ref,) + tuple(held[2:])
     writes = [
         pltpu.make_async_copy(src, dst, sem.at[1, i])
-        for i, (src, dst) in enumerate(zip(held, results))
+        for i, (src, dst) in enumerate(zip(sources, results))
     ]
     for read in reads:
         read.start()
-    for read, write in zip(reads, writes):
+    if tail:
+        dx_held[pl.ds(own, tail), :] = jnp.zeros((tail, dx_held.shape[1]), jnp.bfloat16)
+    reads[0].wait()
+    reads[1].wait()
+    dx_ref[...] = matmul(combine_held[...], dx_held[...]).astype(jnp.bfloat16)
+    writes[0].start()
+    for read, write in zip(reads[2:], writes[1:]):
         read.wait()
         write.start()
     for write in writes:
@@ -427,16 +438,17 @@
     bf16, f32 = jnp.bfloat16, jnp.float32
     hbm = pl.BlockSpec(memory_space=pltpu.HBM)
     work = 2 * units * features * (6 * own + 3 * everyone + 3 * own)
-    results = pl.pallas_call(
+    made_out, dx_back, combine, *others = pl.pallas_call(
         functools.partial(kernel, n, capacity),
         out_shape=(
             jax.ShapeDtypeStruct((tok, features), bf16),
-            jax.ShapeDtypeStruct((tok, features), bf16),
+            jax.ShapeDtypeStruct((own, features), bf16),
+            jax.ShapeDtypeStruct((tok, padded), bf16),
             jax.ShapeDtypeStruct((1, tok), f32),
         )
         + (jax.ShapeDtypeStruct((units, width), bf16),) * 3,
         in_specs=[hbm] * 7,
-        out_specs=(hbm,) * 6,
+        out_specs=(hbm,) * 7,
         scratch_shapes=[
             pltpu.VMEM((tok, features), bf16),
             pltpu.VMEM((1, tok), jnp.int32),
@@ -460,15 +472,14 @@
             pltpu.VMEM((own, features), bf16),
             pltpu.VMEM((own, features), bf16),
             pltpu.VMEM((padded, features), bf16),
-            pltpu.VMEM((padded, features), bf16),
             pltpu.VMEM((tok, features), bf16),
-            pltpu.VMEM((tok, features), bf16),
+            pltpu.VMEM((tok, padded), bf16),
             pltpu.VMEM((1, tok), f32),
             pltpu.VMEM((units, width), bf16),
             pltpu.VMEM((units, width), bf16),
             pltpu.VMEM((units, width), bf16),
             pltpu.SemaphoreType.DMA((7,)),
-            pltpu.SemaphoreType.DMA((6,)),
+            pltpu.SemaphoreType.DMA((7,)),
             pltpu.SemaphoreType.DMA((2, n)),
             pltpu.SemaphoreType.DMA((2, n)),
             pltpu.SemaphoreType.DMA((2, 3, n)),
@@ -491,15 +502,18 @@
         w_up[0],
         w_down[0],
     )
-    layer_out, d_tokens, d_gate, *grads = pl.pallas_call(
+    finished = jax.ShapeDtypeStruct((tok, features), bf16)
+    d_tokens, layer_out, d_gate, *grads = pl.pallas_call(
         write_out,
-        out_shape=tuple(jax.ShapeDtypeStruct(r.shape, r.dtype) for r in results),
-        in_specs=[hbm] * 6,
+        out_shape=(finished,)
+        + tuple(jax.ShapeDtypeStruct(r.shape, r.dtype) for r in (made_out, *others)),
+        in_specs=[hbm] * 7,
         out_specs=(hbm,) * 6,
-        scratch_shapes=[pltpu.VMEM(r.shape, r.dtype) for r in results]
-        + [pltpu.SemaphoreType.DMA((2, 6))],
+        scratch_shapes=[pltpu.VMEM((padded, features), bf16)]
+        + [pltpu.VMEM(r.shape, r.dtype) for r in (combine, made_out, *others)]
+        + [pltpu.VMEM((tok, features), bf16), pltpu.SemaphoreType.DMA((2, 7))],
         compiler_params=pltpu.CompilerParams(vmem_limit_bytes=60 * 1024 * 1024),
-    )(*results)
+    )(dx_back, combine, made_out, *others)
     return (layer_out, d_tokens, d_gate.reshape(tok, 1), *(grad[None] for grad in grads))
 
 

time: 47.4 us -> 47.4 us (level)
  no operation moved by 1% of the time
where the time goes in v5:
time: 47.4 us; the launch traced here: 47.3 us
  Pallas kernels  46.6 us (98%)
  between operations  0.64 us (1%)
    pallas_call x1, Pallas kernels, fused(): pl.pallas_call(functools.partial(kernel, n, capacity), out_shape=(jax.Sha...  44.1 us
    pallas_call x1, Pallas kernels, fused(): pl.pallas_call(write_out, out_shape=(finished,) + tuple((jax.ShapeDtypeSt...  2.54 us

profile of v5, /device:TPU:0, one launch (start us, length us, event | category | flops | bytes accessed | tf_op | source)
XLA Modules:
  0.0 47.3 jit_solution(10024853133435670495)
XLA Ops:
  0.6 44.1 %shard_map.118 = (bf16[128,1024]{1,0:T(8,128)(2,1)}, bf16[192,1024]{1,0:T(8,128)(2,1)}, bf16[128,256]{1,0:T(8,128)(2,1)}, f32[1,128]{1,0:T(1,128)}, bf16[768,256...) custom-call(bf16[128,1024]{1,0:T(8,128)(2,1)} %tokens_hbm.1, s32[1,128]{1,0:T(1,128)} %bitcast.15, ...), custom_call_target="tpu_custom_call" | custom-call | flops 6341787648 | bytes 4718592 | tf_op jit(solution)/shard_map/pallas_call | solution.py:441
  44.7 2.5 %shard_map.119 = (bf16[128,1024]{1,0:T(8,128)(2,1)}, bf16[128,1024]{1,0:T(8,128)(2,1)}, f32[1,128]{1,0:T(1,128)}, bf16[768,256]{1,0:T(8,128)(2,1)}, bf16[768,256]{1,0:T(8,128)(2,1)}, /*index=5*/bf16[768,256]{1,0:T(8,128)(2,1)}) custom-call(bf16[192,1024]{1,0:T(8,128)(2,1)} %get-tuple-element.19.refs_0_, bf16[128,256]{1,0:T(8,128)(2,1)} %get-tuple-element.20.refs_1_, ...), custom_call_target="tpu_custom_call" | custom-call | tf_op jit(solution)/shard_map/pallas_call | solution.py:506
